TPU v7x, 128 devices: a whole 4x4x4 slice. The times are simulated.
128 devices in a mesh: clip: 4 (over z_hi, core), tm: 32 (over x, z_lo, y).
Axes of the slice: x: 4, y: 4, z: 4 (z_hi: 2, z_lo: 2; z = z_hi * 2 + z_lo), core: 2. Of those that a mesh axis runs over, the one named last changes fastest.
Arguments:
- clips: bfloat16 [16, 32, 128, 1024], P('clip', 'tm'), may hold values from -6 to 6
- w_qkv: bfloat16 [1024, 3072], replicated, may hold values from -8 to 8
- w_out: bfloat16 [1024, 1024], replicated, may hold values from -0.1875 to 0.1875
- cotangent: bfloat16 [16, 32, 128, 1024], P('clip', 'tm'), may hold values from -6 to 6
Outputs:
- grad_clips: bfloat16 [16, 32, 128, 1024], P('clip', 'tm')
- grad_qkv: float32 [1024, 3072], P(('clip', 'tm'))
- grad_out: float32 [1024, 1024], P(('clip', 'tm'))
All inputs are finite; a program needn't handle non-finite values.
Results may differ from a plain program's by a relative error of at most 0.0093.
Values may be sent and summed in bfloat16 or wider, within the bound.
A program may use at most 128 MiB of HBM per device.

v0:
```python
import jax
import jax.numpy as jnp
from jax import lax
from jax.experimental import pallas as pl
from jax.experimental.pallas import tpu as pltpu
from jax.sharding import PartitionSpec as P

D = 1024
WIDTH = 64
PAIRS = 8
FRAMES = 32
PATCHES = 16
ROWS = FRAMES * PATCHES
GROUP = 128
GROUPS = ROWS // GROUP
EPSILON = 1e-06
SCALING = WIDTH ** (-0.5)
NEGATIVE = -1e30
F32 = jnp.float32
BF16 = jnp.bfloat16
MESH = pl.DeviceIdType.MESH
DIGITS = ("x1", "y1", "z1", "x0", "y0", "z0")
CHUNKS = ((0, 1, 2, 3), (4, 5, 6, 7, 8, 9), (10, 11, 12, 13, 14, 15))
STREAMS = 16


def order_of(stream):
    start = stream if stream < 4 else stream - 4
    return tuple(DIGITS[(start + k) % 6] for k in range(6))


def dot(left, right):
    return jnp.dot(left, right, preferred_element_type=F32)


def dot_nt(left, right):
    return lax.dot_general(left, right, (((1,), (1,)), ((), ())), preferred_element_type=F32)


def dot_tn(left, right):
    return lax.dot_general(left, right, (((0,), (0,)), ((), ())), preferred_element_type=F32)


def kernel(
    clips, w_qkv, w_out, cotangent, out, grad_qkv, grad_out,
    clips_in, cot_in, wq, wo, perm, perm_back, unit, inverse, normed, cot, cot_other, packed, weights,
    mixed, mixed_t, mixed_t_other, normed_t, normed_t_other, mixed_grad, back, back_other,
    partial, arrived, grads, leaving, normed_grad,
    local_sem, send_sem, recv_sem, core_send, core_recv, sum_send, sum_recv,
):
    clip, tm = lax.axis_index("clip"), lax.axis_index("tm")
    z_hi, core = clip // 2, clip % 2
    x, z_lo, y = tm // 8, (tm // 4) % 2, tm % 4

    def shifted(k):
        return ((x + k // 8) % 4) * 8 + ((z_lo + (k // 4) % 2) % 2) * 4 + (y + k % 4) % 4

    def tm_of(x, z_lo, y):
        return x * 8 + z_lo * 4 + y

    other_core = {"clip": z_hi * 2 + 1 - core, "tm": tm}
    partner = {
        "x1": {"clip": clip, "tm": tm_of(3 - x, z_lo, y)},
        "x0": {"clip": clip, "tm": tm_of(x + 1 - 2 * (x % 2), z_lo, y)},
        "y1": {"clip": clip, "tm": tm_of(x, z_lo, 3 - y)},
        "y0": {"clip": clip, "tm": tm_of(x, z_lo, y + 1 - 2 * (y % 2))},
        "z1": {"clip": (1 - z_hi) * 2 + core, "tm": tm_of(x, 1 - z_lo, y)},
        "z0": {"clip": clip, "tm": tm_of(x, 1 - z_lo, y)},
    }
    digit = {
        "x1": x // 2, "x0": (x // 2 + x) % 2, "y1": y // 2, "y0": (y // 2 + y) % 2,
        "z1": z_hi, "z0": (z_hi + z_lo) % 2,
    }

    locals_ = [
        pltpu.make_async_copy(w_qkv, wq, local_sem.at[0]),
        pltpu.make_async_copy(w_out, wo, local_sem.at[1]),
        pltpu.make_async_copy(clips.at[tm], clips_in.at[tm], local_sem.at[2]),
        pltpu.make_async_copy(cotangent.at[tm], cot_in.at[tm], local_sem.at[3]),
    ]
    for copy in locals_:
        copy.start()

    barrier = pltpu.get_barrier_semaphore()

    @pl.loop(1, FRAMES)
    def _(k):
        pl.semaphore_signal(barrier, inc=1, device_id={"clip": clip, "tm": shifted(k)}, device_id_type=MESH)

    pl.semaphore_signal(barrier, inc=1, device_id=other_core, device_id_type=MESH)
    pl.semaphore_signal(barrier, inc=1, device_id=partner["z1"], device_id_type=MESH)
    pl.semaphore_wait(barrier, FRAMES + 1)

    def exchange(which, source, target, k):
        there = shifted(k)
        return pltpu.make_async_remote_copy(
            src_ref=source.at[there], dst_ref=target.at[tm],
            send_sem=send_sem.at[which, there], recv_sem=recv_sem.at[which, tm],
            device_id={"clip": clip, "tm": there}, device_id_type=MESH,
        )

    def arrival(which, source, target, k):
        there = shifted(k)
        return pltpu.make_async_remote_copy(
            src_ref=source.at[there], dst_ref=target.at[there],
            send_sem=send_sem.at[which, there], recv_sem=recv_sem.at[which, there],
            device_id={"clip": clip, "tm": there}, device_id_type=MESH,
        )

    def start_all(which, source, target):
        @pl.loop(1, FRAMES)
        def _(k):
            exchange(which, source, target, k).start()

    def wait_all(which, source, target):
        @pl.loop(1, FRAMES)
        def _(k):
            arrival(which, source, target, k).wait_recv()

    def sent_all(which, source, target):
        @pl.loop(1, FRAMES)
        def _(k):
            exchange(which, source, target, k).wait_send()

    def to_core(index, source, target):
        return pltpu.make_async_remote_copy(
            src_ref=source, dst_ref=target, send_sem=core_send.at[index], recv_sem=core_recv.at[index],
            device_id=other_core, device_id_type=MESH,
        )

    normed_copies = [to_core(z, normed_t.at[2 * z + 1 - core], normed_t_other.at[z]) for z in range(2)]
    mixed_copies = [to_core(2 + z, mixed_t.at[2 * z + 1 - core], mixed_t_other.at[z]) for z in range(2)]
    cot_copy = to_core(4, cot, cot_other)
    back_copies = [to_core(5 + h, back.at[h], back_other.at[h]) for h in range(2)]
    core_copies = normed_copies + mixed_copies + [cot_copy] + back_copies

    start_all(0, clips, clips_in)
    start_all(1, cotangent, cot_in)

    row = lax.broadcasted_iota(jnp.int32, (ROWS, ROWS), 0)
    column = lax.broadcasted_iota(jnp.int32, (ROWS, ROWS), 1)
    perm[...] = jnp.where((row & 31) * PATCHES + (row >> 5) == column, 1.0, 0.0).astype(BF16)
    perm_back[...] = jnp.where((column & 31) * PATCHES + (column >> 5) == row, 1.0, 0.0).astype(BF16)
    lane = lax.broadcasted_iota(jnp.int32, (GROUP, GROUP), 1)
    low_half = lane < WIDTH
    low_mask = jnp.where(low_half, 1.0, 0.0).astype(BF16)
    high_mask = jnp.where(low_half, 0.0, 1.0).astype(BF16)
    same = (lax.broadcasted_iota(jnp.int32, (2 * GROUP, GROUP), 0) & (GROUP - 1)) >> 5 == (
        lax.broadcasted_iota(jnp.int32, (2 * GROUP, GROUP), 1) >> 5
    )

    def both(array):
        return jnp.concatenate([array * low_mask, array * high_mask], axis=0)

    def join(array):
        return jnp.where(low_half, array[:GROUP], array[GROUP:]).astype(BF16)

    locals_[2].wait()
    wait_all(0, clips, clips_in)

    @pl.loop(0, 4)
    def _(n):
        columns = pl.ds(pl.multiple_of(n * 256, 256), 256)
        unit[:, columns] = dot(perm[...], clips_in[:, :, columns].reshape(ROWS, 256))

    @pl.loop(0, ROWS // 32)
    def _(r):
        rows = pl.ds(pl.multiple_of(r * 32, 32), 32)
        values = unit[rows, :]
        centred = values - jnp.mean(values, axis=-1, keepdims=True)
        scale = lax.rsqrt(jnp.mean(centred * centred, axis=-1, keepdims=True) + EPSILON)
        result = centred * scale
        unit[rows, :] = result
        normed[rows, :] = result.astype(BF16)
        inverse[rows, :] = jnp.broadcast_to(scale, (32, 128))

    for z in range(4):
        normed_t[z] = normed[:, z * 256 : (z + 1) * 256].T
    for copy in normed_copies:
        copy.start()

    locals_[0].wait()

    @pl.loop(0, 12)
    def _(n):
        columns = pl.ds(pl.multiple_of(n * 256, 256), 256)
        packed[:, columns] = dot(normed[...], wq[:, columns]).astype(BF16)

    @pl.loop(0, GROUPS)
    def _(g):
        rows = pl.ds(pl.multiple_of(g * GROUP, GROUP), GROUP)
        for j in range(PAIRS):
            queries = both(packed[rows, j * 128 : (j + 1) * 128])
            keys = packed[rows, D + j * 128 : D + (j + 1) * 128]
            values = packed[rows, 2 * D + j * 128 : 2 * D + (j + 1) * 128]
            scores = jnp.where(same, dot_nt(queries, keys) * SCALING, NEGATIVE)
            expo = jnp.exp(scores - jnp.max(scores, axis=-1, keepdims=True))
            full = expo / jnp.sum(expo, axis=-1, keepdims=True)
            weights[g, j] = full
            mixed[rows, j * 128 : (j + 1) * 128] = join(dot(full.astype(BF16), values))

    for z in range(4):
        mixed_t[z] = mixed[:, z * 256 : (z + 1) * 256].T
    for copy in mixed_copies:
        copy.start()

    locals_[3].wait()
    wait_all(1, cotangent, cot_in)

    @pl.loop(0, 4)
    def _(n):
        columns = pl.ds(pl.multiple_of(n * 256, 256), 256)
        cot[:, columns] = dot(perm[...], cot_in[:, :, columns].reshape(ROWS, 256)).astype(BF16)

    cot_copy.start()
    locals_[1].wait()

    @pl.loop(0, 4)
    def _(n):
        columns = pl.ds(pl.multiple_of(n * 256, 256), 256)
        mixed_grad[:, columns] = dot_nt(cot[...], wo[columns, :]).astype(BF16)

    def attention_back(half):
        @pl.loop(0, GROUPS)
        def _(g):
            rows = pl.ds(pl.multiple_of(g * GROUP, GROUP), GROUP)
            for local in range(PAIRS // 2):
                j = half * (PAIRS // 2) + local
                queries = both(packed[rows, j * 128 : (j + 1) * 128])
                keys = packed[rows, D + j * 128 : D + (j + 1) * 128]
                values = packed[rows, 2 * D + j * 128 : 2 * D + (j + 1) * 128]
                heads = both(mixed_grad[rows, j * 128 : (j + 1) * 128])
                full = weights[g, j]
                dots = dot_nt(heads, values)
                score = full * (dots - jnp.sum(full * dots, axis=-1, keepdims=True))
                score = (score * SCALING).astype(BF16)
                c = local * 128
                back[half, rows, c : c + 128] = join(dot(score, keys))
                back[half, rows, 512 + c : 640 + c] = dot_tn(score, queries).astype(BF16)
                back[half, rows, 1024 + c : 1152 + c] = dot_tn(full.astype(BF16), heads).astype(BF16)

    def block_index(stream):
        order = order_of(stream)

        def place(names, bits, base):
            total = 0
            for k, name in enumerate(names):
                total = total + ((digit[name] + bits[k]) % 2) * (1 << (base - k))
            return total

        cache = {}

        def index(z_hi_, x_, z_lo_, y_):
            gray = {"x1": x_ >> 1, "x0": (x_ >> 1) ^ (x_ & 1), "y1": y_ >> 1, "y0": (y_ >> 1) ^ (y_ & 1),
                    "z1": z_hi_, "z0": z_hi_ ^ z_lo_}
            bits = tuple(gray[name] for name in order)
            for key, names, base in ((bits[:3] + (0,), order[:3], 5), (bits[3:] + (1,), order[3:], 2)):
                if key not in cache:
                    cache[key] = place(names, key, base)
            return cache[bits[:3] + (0,)] + cache[bits[3:] + (1,)]

        return index

    def product(stream, left, left_other, right, right_other):
        index = block_index(stream)
        for z in range(2):
            total = dot(left[2 * z + core], right) + dot(left_other[z], right_other)
            for n in range(32):
                block = total[n * 8 : n * 8 + 8]
                tile = jnp.concatenate([block[:, :128], block[:, 128:]], axis=0).astype(BF16)
                partial[stream, index(z, n // 8, (n // 4) % 2, n % 4)] = tile

    def sum_copy(stream, step):
        half = 1 << (5 - step)
        return pltpu.make_async_remote_copy(
            src_ref=partial.at[stream, pl.ds(half, half)], dst_ref=arrived.at[stream, pl.ds(half, half)],
            send_sem=sum_send.at[stream, step], recv_sem=sum_recv.at[stream, step],
            device_id=partner[order_of(stream)[step]], device_id_type=MESH,
        )

    def start_sum(chunk):
        for stream in CHUNKS[chunk]:
            sum_copy(stream, 0).start()

    def advance(chunk, step):
        half = 1 << (5 - step)
        for stream in CHUNKS[chunk]:
            sum_copy(stream, step).wait_recv()
            total = partial[stream, :half].astype(F32) + arrived[stream, half : 2 * half].astype(F32)
            if step < 5:
                partial[stream, :half] = total.astype(BF16)
                sum_copy(stream, step + 1).start()
            else:
                c = stream * 256 if chunk == 0 else column_of(stream)
                target = grad_out if chunk == 0 else grad_qkv
                target[:, c : c + 128] = total[0, :8]
                target[:, c + 128 : c + 256] = total[0, 8:]

    def column_of(stream):
        half, n = (stream - 4) // 6, (stream - 4) % 6
        return (n // 2) * D + half * 512 + (n % 2) * 256

    def qkv_products(half):
        back_copies[half].wait_recv()
        for n, stream in enumerate(CHUNKS[1 + half]):
            columns = slice(n * 256, (n + 1) * 256)
            product(stream, normed_t, normed_t_other, back[half, :, columns], back_other[half, :, columns])

    attention_back(0)
    back_copies[0].start()
    for copy in mixed_copies + [cot_copy]:
        copy.wait_recv()
    for stream in CHUNKS[0]:
        columns = slice(stream * 256, (stream + 1) * 256)
        product(stream, mixed_t, mixed_t_other, cot[:, columns], cot_other[:, columns])
    start_sum(0)
    attention_back(1)
    back_copies[1].start()
    advance(0, 0)
    for copy in normed_copies:
        copy.wait_recv()
    qkv_products(0)
    start_sum(1)
    advance(0, 1)

    @pl.loop(0, 4)
    def _(n):
        columns = pl.ds(pl.multiple_of(n * 256, 256), 256)
        total = jnp.zeros((ROWS, 256), F32)
        for half in range(2):
            for part in range(3):
                start = part * D + half * 512
                total += dot_nt(back[half, :, part * 512 : part * 512 + 512], wq[columns, start : start + 512])
        normed_grad[:, columns] = total

    advance(0, 2)
    advance(1, 0)

    @pl.loop(0, ROWS // 32)
    def _(r):
        rows = pl.ds(pl.multiple_of(r * 32, 32), 32)
        gradient = normed_grad[rows, :]
        values = unit[rows, :]
        scale = inverse[rows, :][:, :1]
        gradient = scale * (
            gradient
            - jnp.mean(gradient, axis=-1, keepdims=True)
            - values * jnp.mean(gradient * values, axis=-1, keepdims=True)
        )
        grads[rows, :] = (cot[rows, :].astype(F32) + gradient).astype(BF16)

    @pl.loop(0, 4)
    def _(n):
        columns = pl.ds(pl.multiple_of(n * 256, 256), 256)
        leaving[:, :, columns] = dot(perm_back[...], grads[:, columns]).astype(BF16).reshape(FRAMES, PATCHES, 256)

    own = pltpu.make_async_copy(leaving.at[tm], out.at[tm], local_sem.at[4])
    own.start()
    start_all(2, leaving, out)
    advance(0, 3)
    advance(1, 1)
    qkv_products(1)
    start_sum(2)
    advance(0, 4)
    advance(1, 2)
    advance(2, 0)
    advance(0, 5)
    advance(1, 3)
    advance(2, 1)
    advance(1, 4)
    advance(2, 2)
    advance(1, 5)
    advance(2, 3)
    advance(2, 4)
    advance(2, 5)
    own.wait()
    wait_all(2, leaving, out)
    sent_all(0, clips, clips_in)
    sent_all(1, cotangent, cot_in)
    sent_all(2, leaving, out)
    for copy in core_copies:
        copy.wait_send()
    for stream in range(STREAMS):
        for step in range(6):
            sum_copy(stream, step).wait_send()


def shards(clips, w_qkv, w_out, cotangent):
    any_ = pl.BlockSpec(memory_space=pl.ANY)
    vmem = pl.BlockSpec(memory_space=pltpu.VMEM)
    blocks = (FRAMES, PATCHES, D)
    out, grad_qkv, grad_out = pl.pallas_call(
        kernel,
        out_shape=(
            jax.ShapeDtypeStruct(blocks, BF16),
            jax.ShapeDtypeStruct((8, 3 * D), F32),
            jax.ShapeDtypeStruct((8, D), F32),
        ),
        in_specs=[any_] * 4,
        out_specs=(any_, vmem, vmem),
        scratch_shapes=[
            pltpu.VMEM(blocks, BF16),
            pltpu.VMEM(blocks, BF16),
            pltpu.VMEM((D, 3 * D), BF16),
            pltpu.VMEM((D, D), BF16),
            pltpu.VMEM((ROWS, ROWS), BF16),
            pltpu.VMEM((ROWS, ROWS), BF16),
            pltpu.VMEM((ROWS, D), F32),
            pltpu.VMEM((ROWS, 128), F32),
            pltpu.VMEM((ROWS, D), BF16),
            pltpu.VMEM((ROWS, D), BF16),
            pltpu.VMEM((ROWS, D), BF16),
            pltpu.VMEM((ROWS, 3 * D), BF16),
            pltpu.VMEM((GROUPS, PAIRS, 2 * GROUP, GROUP), F32),
            pltpu.VMEM((ROWS, D), BF16),
            pltpu.VMEM((4, 256, ROWS), BF16),
            pltpu.VMEM((2, 256, ROWS), BF16),
            pltpu.VMEM((4, 256, ROWS), BF16),
            pltpu.VMEM((2, 256, ROWS), BF16),
            pltpu.VMEM((ROWS, D), BF16),
            pltpu.VMEM((2, ROWS, 1536), BF16),
            pltpu.VMEM((2, ROWS, 1536), BF16),
            pltpu.VMEM((STREAMS, 64, 16, 128), BF16),
            pltpu.VMEM((STREAMS, 64, 16, 128), BF16),
            pltpu.VMEM((ROWS, D), BF16),
            pltpu.VMEM(blocks, BF16),
            pltpu.VMEM((ROWS, D), F32),
            pltpu.SemaphoreType.DMA((5,)),
            pltpu.SemaphoreType.DMA((3, FRAMES)),
            pltpu.SemaphoreType.DMA((3, FRAMES)),
            pltpu.SemaphoreType.DMA((7,)),
            pltpu.SemaphoreType.DMA((7,)),
            pltpu.SemaphoreType.DMA((STREAMS, 6)),
            pltpu.SemaphoreType.DMA((STREAMS, 6)),
        ],
        compiler_params=pltpu.CompilerParams(
            collective_id=0, has_side_effects=True, vmem_limit_bytes=60 * 1024 * 1024
        ),
        cost_estimate=pl.CostEstimate(flops=12 * 10**9, bytes_accessed=12 * 2**20, transcendentals=2**20),
    )(clips.reshape(blocks), w_qkv, w_out, cotangent.reshape(blocks))
    return out.reshape(clips.shape), grad_qkv, grad_out


def solution(mesh):
    return jax.shard_map(
        shards,
        mesh=mesh,
        in_specs=(P("clip", "tm", None, None), P(), P(), P("clip", "tm", None, None)),
        out_specs=(P("clip", "tm", None, None), P(("clip", "tm"), None), P(("clip", "tm"), None)),
        check_vma=False,
    )
```

profile of v0, /device:TPU:0, one launch (start us, length us, event | category | flops | bytes accessed | tf_op | source)
XLA Modules:
  0.0 115.7 jit_solution(1444725597517048333)
XLA Ops:
  0.6 109.9 %shard_map.67 = (bf16[32,16,1024]{2,1,0:T(8,128)(2,1)}, f32[8,3072]{1,0:T(8,128)}, f32[8,1024]{1,0:T(8,128)}) custom-call(bf16[32,16,1024]{2,1,0:T(8,128)(2,1)} %bitcast.6, bf16[1024,3072]{1,0:T(8,128)(2,1)} %w_qkv.1, bf16[1024,1024]{1,0:T(8,128)(2,1)} %w_out.1, bf16[32,16,1024]{2,1,0:T(8,128)(2,1)} %bitcast.7), custom_call_target="tpu_custom_call" | custom-call | flops 12000000000 | bytes 12582912 | tf_op jit(solution)/shard_map/pallas_call | solution.py:392
  110.6 2.3 %copy.11 = bf16[4,1,128,1024]{3,2,1,0:T(8,128)(2,1)} copy(bf16[4,1,128,1024]{3,2,1,0:T(8,128)(2,1)} %bitcast.5) | data formatting | bytes 2097152
  112.8 1.5 %copy.12 = f32[8,3072]{1,0:T(8,128)} copy(f32[8,3072]{1,0:T(8,128)} %get-tuple-element.16) | data formatting | bytes 196608
  114.4 1.4 %copy.13 = f32[8,1024]{1,0:T(8,128)} copy(f32[8,1024]{1,0:T(8,128)} %get-tuple-element.17) | data formatting | bytes 65536
where the time goes:
time: 116 us
  Pallas kernels  110 us (95%)
  local copies, waits for them, and re-layouts  5.18 us (4%)
    pallas_call x1, Pallas kernels, shards(): pl.pallas_call(kernel, out_shape=(jax.ShapeDtypeStruct(blocks, BF16), jax...  110 us
    unnamed x3, local copies, waits for them, and re-layouts  5.18 us

commit v1 on v0

v1 whole, which is shorter than its diff:
```python
import jax
import jax.numpy as jnp
from jax import lax
from jax.experimental import pallas as pl
from jax.experimental.pallas import tpu as pltpu
from jax.sharding import PartitionSpec as P

D = 1024
WIDTH = 64
PAIRS = 8
FRAMES = 32
PATCHES = 16
ROWS = FRAMES * PATCHES
GROUP = 128
GROUPS = ROWS // GROUP
EPSILON = 1e-06
SCALING = WIDTH ** (-0.5)
NEGATIVE = -1e30
F32 = jnp.float32
BF16 = jnp.bfloat16
MESH = pl.DeviceIdType.MESH
AXES = ("x", "y", "z")
CHUNKS = ((0, 1, 2, 3), (4, 5, 6), (7, 8, 9), (10, 11, 12), (13, 14, 15))
STREAMS = 16
QUARTERS = 4
GATE = 8


def order_of(stream):
    return tuple(AXES[(stream + k) % 3] for k in range(3))


def dot(left, right):
    return jnp.dot(left, right, preferred_element_type=F32)


def dot_nt(left, right):
    return lax.dot_general(left, right, (((1,), (1,)), ((), ())), preferred_element_type=F32)


def dot_tn(left, right):
    return lax.dot_general(left, right, (((0,), (0,)), ((), ())), preferred_element_type=F32)


def kernel(
    clips, w_qkv, w_out, cotangent, out, grad_qkv, grad_out,
    clips_in, cot_in, wq, wo, perm, perm_back, unit, inverse, normed, cot, cot_other, packed, weights,
    mixed_t, mixed_t_other, normed_t, normed_t_other, mixed_grad, back, back_other,
    partial, arrived, grads, leaving, normed_grad,
    local_sem, send_sem, recv_sem, core_send, core_recv, sum_send, sum_recv,
):
    clip, tm = lax.axis_index("clip"), lax.axis_index("tm")
    z_hi, core = clip // 2, clip % 2
    x, z_lo, y = tm // 8, (tm // 4) % 2, tm % 4

    def shifted(k):
        return ((x + k // 8) % 4) * 8 + ((z_lo + (k // 4) % 2) % 2) * 4 + (y + k % 4) % 4

    def tm_of(x, z_lo, y):
        return x * 8 + z_lo * 4 + y

    other_core = {"clip": z_hi * 2 + 1 - core, "tm": tm}
    place = {"x": x, "y": y, "z": z_hi * 2 + z_lo}

    def along(axis, step):
        if axis == "x":
            return {"clip": clip, "tm": tm_of((x + step) % 4, z_lo, y)}
        if axis == "y":
            return {"clip": clip, "tm": tm_of(x, z_lo, (y + step) % 4)}
        there = (place["z"] + step) % 4
        return {"clip": there // 2 * 2 + core, "tm": tm_of(x, there % 2, y)}

    locals_ = [
        pltpu.make_async_copy(w_qkv, wq, local_sem.at[0]),
        pltpu.make_async_copy(w_out, wo, local_sem.at[1]),
        pltpu.make_async_copy(clips.at[tm], clips_in.at[tm], local_sem.at[2]),
        pltpu.make_async_copy(cotangent.at[tm], cot_in.at[tm], local_sem.at[3]),
    ]
    for copy in locals_:
        copy.start()

    barrier = pltpu.get_barrier_semaphore()

    for k in range(1, FRAMES):
        pl.semaphore_signal(barrier, inc=1, device_id={"clip": clip, "tm": shifted(k)}, device_id_type=MESH)

    pl.semaphore_signal(barrier, inc=1, device_id=other_core, device_id_type=MESH)
    for step in range(1, 4):
        pl.semaphore_signal(barrier, inc=1, device_id=along("z", step), device_id_type=MESH)
    pl.semaphore_wait(barrier, FRAMES + 3)

    def exchange(which, source, target, k):
        there = shifted(k)
        return pltpu.make_async_remote_copy(
            src_ref=source.at[there], dst_ref=target.at[tm],
            send_sem=send_sem.at[which, there], recv_sem=recv_sem.at[which, tm],
            device_id={"clip": clip, "tm": there}, device_id_type=MESH,
        )

    def arrival(which, source, target, k):
        there = shifted(k)
        return pltpu.make_async_remote_copy(
            src_ref=source.at[there], dst_ref=target.at[there],
            send_sem=send_sem.at[which, there], recv_sem=recv_sem.at[which, there],
            device_id={"clip": clip, "tm": there}, device_id_type=MESH,
        )

    def start_all(which, source, target):
        @pl.loop(1, FRAMES)
        def _(k):
            exchange(which, source, target, k).start()

    def wait_all(which, source, target, first=1, last=FRAMES):
        @pl.loop(first, last)
        def _(k):
            arrival(which, source, target, k).wait_recv()

    def sent_all(which, source, target):
        @pl.loop(1, FRAMES)
        def _(k):
            exchange(which, source, target, k).wait_send()

    def to_core(index, source, target):
        return pltpu.make_async_remote_copy(
            src_ref=source, dst_ref=target, send_sem=core_send.at[index], recv_sem=core_recv.at[index],
            device_id=other_core, device_id_type=MESH,
        )

    normed_copies = [to_core(z, normed_t.at[2 * z + 1 - core], normed_t_other.at[z]) for z in range(2)]
    mixed_copies = [to_core(2 + z, mixed_t.at[2 * z + 1 - core], mixed_t_other.at[z]) for z in range(2)]
    cot_copy = to_core(4, cot, cot_other)
    back_columns = [[pl.ds(part * D + q * 256, 256) for part in range(3)] for q in range(QUARTERS)]
    back_copies = [
        [to_core(5 + q * 3 + n, back.at[:, columns], back_other.at[:, columns]) for n, columns in enumerate(back_columns[q])]
        for q in range(QUARTERS)
    ]
    core_copies = normed_copies + mixed_copies + [cot_copy] + sum(back_copies, [])

    start_all(0, clips, clips_in)
    row = lax.broadcasted_iota(jnp.int32, (ROWS, ROWS), 0)
    column = lax.broadcasted_iota(jnp.int32, (ROWS, ROWS), 1)
    perm[...] = jnp.where((row & 31) * PATCHES + (row >> 5) == column, 1.0, 0.0).astype(BF16)
    perm_back[...] = jnp.where((column & 31) * PATCHES + (column >> 5) == row, 1.0, 0.0).astype(BF16)
    lane = lax.broadcasted_iota(jnp.int32, (GROUP, GROUP), 1)
    low_half = lane < WIDTH
    same = lax.broadcasted_iota(jnp.int32, (GROUP, 2 * GROUP), 0) >> 5 == (
        lax.broadcasted_iota(jnp.int32, (GROUP, 2 * GROUP), 1) & (GROUP - 1)
    ) >> 5

    def both(array, scale=1.0):
        low_mask = jnp.where(low_half, scale, 0.0).astype(BF16)
        high_mask = jnp.where(low_half, 0.0, scale).astype(BF16)
        return jnp.concatenate([array * low_mask, array * high_mask], axis=0)

    locals_[2].wait()
    wait_all(0, clips, clips_in, 1, GATE)
    start_all(1, cotangent, cot_in)
    wait_all(0, clips, clips_in, GATE)

    unit[...] = dot(perm[...], clips_in[...].reshape(ROWS, D))

    @pl.loop(0, ROWS // 32, unroll=4)
    def _(r):
        rows = pl.ds(pl.multiple_of(r * 32, 32), 32)
        values = unit[rows, :]
        centred = values - jnp.mean(values, axis=-1, keepdims=True)
        scale = lax.rsqrt(jnp.mean(centred * centred, axis=-1, keepdims=True) + EPSILON)
        result = centred * scale
        unit[rows, :] = result
        normed[rows, :] = result.astype(BF16)
        inverse[rows, :] = jnp.broadcast_to(scale, (32, 128))

    for n in range(4):
        normed_t[n] = normed[:, n * 256 : (n + 1) * 256].T
    for copy in normed_copies:
        copy.start()

    locals_[0].wait()

    @pl.loop(0, 3)
    def _(n):
        columns = pl.ds(pl.multiple_of(n * D, D), D)
        packed[:, columns] = dot(normed[...], wq[:, columns]).astype(BF16)

    @pl.loop(0, GROUPS)
    def _(g):
        rows = pl.ds(pl.multiple_of(g * GROUP, GROUP), GROUP)
        for j in range(PAIRS):
            queries = both(packed[rows, j * 128 : (j + 1) * 128], SCALING)
            keys = packed[rows, D + j * 128 : D + (j + 1) * 128]
            values = packed[rows, 2 * D + j * 128 : 2 * D + (j + 1) * 128]
            scores = jnp.where(same, dot_nt(keys, queries), NEGATIVE)
            expo = jnp.exp(scores - jnp.max(scores, axis=0, keepdims=True))
            full = expo * (1.0 / jnp.sum(expo, axis=0, keepdims=True))
            weights[g, j] = full
            result = dot(values.T, full.astype(BF16)).astype(BF16)
            mixed_t[j // 2, (j % 2) * 128 : (j % 2) * 128 + WIDTH, rows] = result[:WIDTH, :GROUP]
            mixed_t[j // 2, (j % 2) * 128 + WIDTH : (j % 2 + 1) * 128, rows] = result[WIDTH:, GROUP:]

    for copy in mixed_copies:
        copy.start()

    locals_[3].wait()
    wait_all(1, cotangent, cot_in)

    cot[...] = dot(perm[...], cot_in[...].reshape(ROWS, D)).astype(BF16)

    cot_copy.start()
    locals_[1].wait()

    mixed_grad[...] = dot_nt(cot[...], wo[...]).astype(BF16)

    def attention_back(quarter):
        @pl.loop(0, GROUPS, unroll=2)
        def _(g):
            rows = pl.ds(pl.multiple_of(g * GROUP, GROUP), GROUP)
            for j in range(quarter * 2, quarter * 2 + 2):
                queries = both(packed[rows, j * 128 : (j + 1) * 128], SCALING)
                keys = packed[rows, D + j * 128 : D + (j + 1) * 128]
                values = packed[rows, 2 * D + j * 128 : 2 * D + (j + 1) * 128]
                heads = both(mixed_grad[rows, j * 128 : (j + 1) * 128])
                full = weights[g, j]
                dots = dot_nt(values, heads)
                score = (full * (dots - jnp.sum(full * dots, axis=0, keepdims=True))).astype(BF16)
                query_grad = dot_tn(score, keys)
                query_grad = jnp.where(low_half, query_grad[:GROUP], query_grad[GROUP:]) * SCALING
                c = j * 128
                back[rows, c : c + 128] = query_grad.astype(BF16)
                back[rows, D + c : D + c + 128] = dot(score, queries).astype(BF16)
                back[rows, 2 * D + c : 2 * D + c + 128] = dot(full.astype(BF16), heads).astype(BF16)

    def product(stream, left, left_other, right, right_other):
        order = order_of(stream)
        offset = [[(n + 4 - place[axis]) % 4 * 4 ** (2 - k) for n in range(4)] for k, axis in enumerate(order)]
        pair = [[first + second for second in offset[1]] for first in offset[0]]
        for half in range(2):
            total = dot(left[2 * half + core], right) + dot(left_other[half], right_other)
            for n in range(32):
                at = {"x": n // 8, "z": half * 2 + (n // 4) % 2, "y": n % 4}
                index = pair[at[order[0]]][at[order[1]]] + offset[2][at[order[2]]]
                block = total[n * 8 : n * 8 + 8]
                tile = jnp.concatenate([block[:, :128], block[:, 128:]], axis=0).astype(BF16)
                partial[stream, index] = tile

    def sum_copy(stream, level, step):
        size = 4 ** (2 - level)
        return pltpu.make_async_remote_copy(
            src_ref=partial.at[stream, pl.ds(step * size, size)], dst_ref=arrived.at[stream, pl.ds(step * size, size)],
            send_sem=sum_send.at[stream, level], recv_sem=sum_recv.at[stream, level],
            device_id=along(order_of(stream)[level], step), device_id_type=MESH,
        )

    def sum_all(stream, level, semaphore):
        blocks = pl.ds(4 ** (2 - level), 3 * 4 ** (2 - level))
        return pltpu.make_async_copy(partial.at[stream, blocks], arrived.at[stream, blocks], semaphore.at[stream, level])

    def start_sum(chunk, level=0):
        for step in (2, 1, 3):
            for stream in CHUNKS[chunk]:
                sum_copy(stream, level, step).start()

    def advance(chunk, level):
        size = 4 ** (2 - level)
        for stream in CHUNKS[chunk]:
            sum_all(stream, level, sum_recv).wait()
            total = partial[stream, :size].astype(F32)
            for step in range(1, 4):
                total += arrived[stream, step * size : (step + 1) * size].astype(F32)
            if level < 2:
                partial[stream, :size] = total.astype(BF16)
            else:
                c = stream * 256 if chunk == 0 else column_of(stream)
                target = grad_out if chunk == 0 else grad_qkv
                target[:, c : c + 128] = total[0, :8]
                target[:, c + 128 : c + 256] = total[0, 8:]
        if level < 2:
            start_sum(chunk, level + 1)

    def column_of(stream):
        return (stream - 4) % 3 * D + (stream - 4) // 3 * 256

    def qkv_products(quarter):
        for copy in back_copies[quarter]:
            copy.wait_recv()
        for columns, stream in zip(back_columns[quarter], CHUNKS[1 + quarter]):
            product(stream, normed_t, normed_t_other, back[:, columns], back_other[:, columns])
        start_sum(1 + quarter)

    def back_quarter(quarter):
        attention_back(quarter)
        for copy in back_copies[quarter]:
            copy.start()

    for copy in mixed_copies + [cot_copy]:
        copy.wait_recv()
    for stream in CHUNKS[0]:
        columns = slice(stream * 256, (stream + 1) * 256)
        product(stream, mixed_t, mixed_t_other, cot[:, columns], cot_other[:, columns])
    start_sum(0)
    back_quarter(0)
    back_quarter(1)
    for copy in normed_copies:
        copy.wait_recv()
    qkv_products(0)
    advance(0, 0)
    back_quarter(2)
    qkv_products(1)
    advance(0, 1)
    back_quarter(3)
    qkv_products(2)
    advance(1, 0)
    qkv_products(3)
    advance(0, 2)
    advance(2, 0)
    normed_grad[:256, :] = dot_nt(back[:256, :], wq[...])
    advance(1, 1)
    normed_grad[256:, :] = dot_nt(back[256:, :], wq[...])
    advance(3, 0)
    advance(2, 1)

    @pl.loop(0, ROWS // 32, unroll=4)
    def _(r):
        rows = pl.ds(pl.multiple_of(r * 32, 32), 32)
        gradient = normed_grad[rows, :]
        values = unit[rows, :]
        scale = inverse[rows, :][:, :1]
        gradient = scale * (
            gradient
            - jnp.mean(gradient, axis=-1, keepdims=True)
            - values * jnp.mean(gradient * values, axis=-1, keepdims=True)
        )
        grads[rows, :] = (cot[rows, :].astype(F32) + gradient).astype(BF16)

    leaving[...] = dot(perm_back[...], grads[...]).astype(BF16).reshape(FRAMES, PATCHES, D)

    advance(4, 0)
    own = pltpu.make_async_copy(leaving.at[tm], out.at[tm], local_sem.at[4])
    own.start()
    start_all(2, leaving, out)
    advance(3, 1)
    advance(4, 1)
    advance(1, 2)
    advance(2, 2)
    advance(3, 2)
    advance(4, 2)
    own.wait()
    wait_all(2, leaving, out)
    sent_all(0, clips, clips_in)
    sent_all(1, cotangent, cot_in)
    sent_all(2, leaving, out)
    for copy in core_copies:
        copy.wait_send()
    for stream in range(STREAMS):
        for level in range(3):
            sum_all(stream, level, sum_send).wait()


def shards(clips, w_qkv, w_out, cotangent):
    any_ = pl.BlockSpec(memory_space=pl.ANY)
    vmem = pl.BlockSpec(memory_space=pltpu.VMEM)
    blocks = (FRAMES, PATCHES, D)
    out, grad_qkv, grad_out = pl.pallas_call(
        kernel,
        out_shape=(
            jax.ShapeDtypeStruct(blocks, BF16),
            jax.ShapeDtypeStruct((8, 3 * D), F32),
            jax.ShapeDtypeStruct((8, D), F32),
        ),
        in_specs=[any_] * 4,
        out_specs=(any_, vmem, vmem),
        scratch_shapes=[
            pltpu.VMEM(blocks, BF16),
            pltpu.VMEM(blocks, BF16),
            pltpu.VMEM((D, 3 * D), BF16),
            pltpu.VMEM((D, D), BF16),
            pltpu.VMEM((ROWS, ROWS), BF16),
            pltpu.VMEM((ROWS, ROWS), BF16),
            pltpu.VMEM((ROWS, D), F32),
            pltpu.VMEM((ROWS, 128), F32),
            pltpu.VMEM((ROWS, D), BF16),
            pltpu.VMEM((ROWS, D), BF16),
            pltpu.VMEM((ROWS, D), BF16),
            pltpu.VMEM((ROWS, 3 * D), BF16),
            pltpu.VMEM((GROUPS, PAIRS, GROUP, 2 * GROUP), F32),
            pltpu.VMEM((4, 256, ROWS), BF16),
            pltpu.VMEM((2, 256, ROWS), BF16),
            pltpu.VMEM((4, 256, ROWS), BF16),
            pltpu.VMEM((2, 256, ROWS), BF16),
            pltpu.VMEM((ROWS, D), BF16),
            pltpu.VMEM((ROWS, 3 * D), BF16),
            pltpu.VMEM((ROWS, 3 * D), BF16),
            pltpu.VMEM((STREAMS, 64, 16, 128), BF16),
            pltpu.VMEM((STREAMS, 64, 16, 128), BF16),
            pltpu.VMEM((ROWS, D), BF16),
            pltpu.VMEM(blocks, BF16),
            pltpu.VMEM((ROWS, D), F32),
            pltpu.SemaphoreType.DMA((5,)),
            pltpu.SemaphoreType.DMA((3, FRAMES)),
            pltpu.SemaphoreType.DMA((3, FRAMES)),
            pltpu.SemaphoreType.DMA((17,)),
            pltpu.SemaphoreType.DMA((17,)),
            pltpu.SemaphoreType.DMA((STREAMS, 3)),
            pltpu.SemaphoreType.DMA((STREAMS, 3)),
        ],
        compiler_params=pltpu.CompilerParams(
            collective_id=0, has_side_effects=True, vmem_limit_bytes=60 * 1024 * 1024
        ),
        cost_estimate=pl.CostEstimate(flops=12 * 10**9, bytes_accessed=12 * 2**20, transcendentals=2**20),
    )(clips.reshape(blocks), w_qkv, w_out, cotangent.reshape(blocks))

    def finish(*refs):
        copies = [pltpu.make_async_copy(refs[i], refs[3 + i], refs[6].at[i]) for i in range(3)]
        for copy in copies:
            copy.start()
        for copy in copies:
            copy.wait()

    out, grad_qkv, grad_out = pl.pallas_call(
        finish,
        out_shape=tuple(jax.ShapeDtypeStruct(a.shape, a.dtype) for a in (out, grad_qkv, grad_out)),
        in_specs=[vmem] * 3,
        out_specs=(any_,) * 3,
        scratch_shapes=[pltpu.SemaphoreType.DMA((3,))],
    )(out, grad_qkv, grad_out)
    return out.reshape(clips.shape), grad_qkv, grad_out


def solution(mesh):
    return jax.shard_map(
        shards,
        mesh=mesh,
        in_specs=(P("clip", "tm", None, None), P(), P(), P("clip", "tm", None, None)),
        out_specs=(P("clip", "tm", None, None), P(("clip", "tm"), None), P(("clip", "tm"), None)),
        check_vma=False,
    )
```

time: 116 us -> 94.7 us (0.82)
  Pallas kernels: 110 us -> 93.5 us
  local copies, waits for them, and re-layouts: 5.18 us -> 0 us
    pallas_call x1, Pallas kernels: 110 us -> 91.2 us  [shards(): pl.pallas_call(kernel, out_shape=(jax.ShapeDtypeStruct(blocks, BF16), jax...]
    unnamed x3 -> x0, local copies, waits for them, and re-layouts: 5.18 us -> none
    pallas_call x0 -> x1, Pallas kernels: none -> 2.3 us  [shards(): pl.pallas_call(finish, out_shape=tuple((jax.ShapeDtypeStruct(a.shape, a.d...]
where the time goes in v1:
time: 94.7 us; the launch traced here: 94.3 us
  Pallas kernels  93.5 us (99%)
    pallas_call x1, Pallas kernels, shards(): pl.pallas_call(kernel, out_shape=(jax.ShapeDtypeStruct(blocks, BF16), jax...  91.2 us
    pallas_call x1, Pallas kernels, shards(): pl.pallas_call(finish, out_shape=tuple((jax.ShapeDtypeStruct(a.shape, a.d...  2.3 us

profile of v1, /device:TPU:0, one launch (start us, length us, event | category | flops | bytes accessed | tf_op | source)
XLA Modules:
  0.0 94.3 jit_solution(806471319876116275)
XLA Ops:
  0.6 91.2 %shard_map.67 = (bf16[32,16,1024]{2,1,0:T(8,128)(2,1)}, f32[8,3072]{1,0:T(8,128)}, f32[8,1024]{1,0:T(8,128)}) custom-call(bf16[32,16,1024]{2,1,0:T(8,128)(2,1)} %bitcast.5, bf16[1024,3072]{1,0:T(8,128)(2,1)} %w_qkv.1, bf16[1024,1024]{1,0:T(8,128)(2,1)} %w_out.1, bf16[32,16,1024]{2,1,0:T(8,128)(2,1)} %bitcast.6), custom_call_target="tpu_custom_call" | custom-call | flops 12000000000 | bytes 12582912 | tf_op jit(solution)/shard_map/pallas_call | solution.py:362
  91.8 2.3 %shard_map.68 = (bf16[32,16,1024]{2,1,0:T(8,128)(2,1)}, f32[8,3072]{1,0:T(8,128)}, f32[8,1024]{1,0:T(8,128)}) custom-call(bf16[32,16,1024]{2,1,0:T(8,128)(2,1)} %get-tuple-element.9.refs_0_, f32[8,3072]{1,0:T(8,128)} %get-tuple-element.10.refs_1_, f32[8,1024]{1,0:T(8,128)} %get-tuple-element.11.refs_2_), custom_call_target="tpu_custom_call" | custom-call | tf_op jit(solution)/shard_map/pallas_call | solution.py:418

commit v2 on v1

--- a/solution.py
+++ b/solution.py
@@ -23,7 +23,7 @@
 CHUNKS = ((0, 1, 2, 3), (4, 5, 6), (7, 8, 9), (10, 11, 12), (13, 14, 15))
 STREAMS = 16
 QUARTERS = 4
-GATE = 8
+GATE = 12
 
 
 def order_of(stream):
@@ -54,7 +54,7 @@
     x, z_lo, y = tm // 8, (tm // 4) % 2, tm % 4
 
     def shifted(k):
-        return ((x + k // 8) % 4) * 8 + ((z_lo + (k // 4) % 2) % 2) * 4 + (y + k % 4) % 4
+        return ((x + k + k // 8) % 4) * 8 + ((z_lo + k // 4 + k) % 2) * 4 + (y + k) % 4
 
     def tm_of(x, z_lo, y):
         return x * 8 + z_lo * 4 + y
@@ -291,33 +291,31 @@
         for copy in back_copies[quarter]:
             copy.start()
 
+    back_quarter(0)
     for copy in mixed_copies + [cot_copy]:
         copy.wait_recv()
     for stream in CHUNKS[0]:
         columns = slice(stream * 256, (stream + 1) * 256)
         product(stream, mixed_t, mixed_t_other, cot[:, columns], cot_other[:, columns])
     start_sum(0)
-    back_quarter(0)
     back_quarter(1)
     for copy in normed_copies:
         copy.wait_recv()
     qkv_products(0)
+    back_quarter(2)
     advance(0, 0)
-    back_quarter(2)
     qkv_products(1)
+    back_quarter(3)
     advance(0, 1)
-    back_quarter(3)
     qkv_products(2)
     advance(1, 0)
+    normed_grad[:256, :] = dot_nt(back[:256, :], wq[...])
     qkv_products(3)
     advance(0, 2)
     advance(2, 0)
-    normed_grad[:256, :] = dot_nt(back[:256, :], wq[...])
+    normed_grad[256:, :] = dot_nt(back[256:, :], wq[...])
     advance(1, 1)
-    normed_grad[256:, :] = dot_nt(back[256:, :], wq[...])
     advance(3, 0)
-    advance(2, 1)
-
     @pl.loop(0, ROWS // 32, unroll=4)
     def _(r):
         rows = pl.ds(pl.multiple_of(r * 32, 32), 32)
@@ -333,13 +331,14 @@
 
     leaving[...] = dot(perm_back[...], grads[...]).astype(BF16).reshape(FRAMES, PATCHES, D)
 
+    advance(2, 1)
     advance(4, 0)
+    advance(3, 1)
     own = pltpu.make_async_copy(leaving.at[tm], out.at[tm], local_sem.at[4])
     own.start()
     start_all(2, leaving, out)
-    advance(3, 1)
+    advance(1, 2)
     advance(4, 1)
-    advance(1, 2)
     advance(2, 2)
     advance(3, 2)
     advance(4, 2)

time: 94.7 us -> 89.3 us (0.943)
  Pallas kernels: 93.5 us -> 88.3 us
    pallas_call x1, Pallas kernels: 91.2 us -> 86 us  [shards(): pl.pallas_call(kernel, out_shape=(jax.ShapeDtypeStruct(blocks, BF16), jax...]
where the time goes in v2:
time: 89.3 us; the launch traced here: 89.1 us
  Pallas kernels  88.3 us (99%)
    pallas_call x1, Pallas kernels, shards(): pl.pallas_call(kernel, out_shape=(jax.ShapeDtypeStruct(blocks, BF16), jax...  86 us
    pallas_call x1, Pallas kernels, shards(): pl.pallas_call(finish, out_shape=tuple((jax.ShapeDtypeStruct(a.shape, a.d...  2.3 us

profile of v2, /device:TPU:0, one launch (start us, length us, event | category | flops | bytes accessed | tf_op | source)
XLA Modules:
  0.0 89.1 jit_solution(5402723379041677697)
XLA Ops:
  0.6 86.0 %shard_map.67 = (bf16[32,16,1024]{2,1,0:T(8,128)(2,1)}, f32[8,3072]{1,0:T(8,128)}, f32[8,1024]{1,0:T(8,128)}) custom-call(bf16[32,16,1024]{2,1,0:T(8,128)(2,1)} %bitcast.5, bf16[1024,3072]{1,0:T(8,128)(2,1)} %w_qkv.1, bf16[1024,1024]{1,0:T(8,128)(2,1)} %w_out.1, bf16[32,16,1024]{2,1,0:T(8,128)(2,1)} %bitcast.6), custom_call_target="tpu_custom_call" | custom-call | flops 12000000000 | bytes 12582912 | tf_op jit(solution)/shard_map/pallas_call | solution.py:361
  86.6 2.3 %shard_map.68 = (bf16[32,16,1024]{2,1,0:T(8,128)(2,1)}, f32[8,3072]{1,0:T(8,128)}, f32[8,1024]{1,0:T(8,128)}) custom-call(bf16[32,16,1024]{2,1,0:T(8,128)(2,1)} %get-tuple-element.9.refs_0_, f32[8,3072]{1,0:T(8,128)} %get-tuple-element.10.refs_1_, f32[8,1024]{1,0:T(8,128)} %get-tuple-element.11.refs_2_), custom_call_target="tpu_custom_call" | custom-call | tf_op jit(solution)/shard_map/pallas_call | solution.py:417

commit v3 on v2

--- a/solution.py
+++ b/solution.py
@@ -23,7 +23,7 @@
 CHUNKS = ((0, 1, 2, 3), (4, 5, 6), (7, 8, 9), (10, 11, 12), (13, 14, 15))
 STREAMS = 16
 QUARTERS = 4
-GATE = 12
+GATE = 15
 
 
 def order_of(stream):

time: 89.3 us -> 90.4 us (1.012)
  Pallas kernels: 88.3 us -> 89.5 us
    pallas_call x1, Pallas kernels: 86 us -> 87.2 us  [shards(): pl.pallas_call(kernel, out_shape=(jax.ShapeDtypeStruct(blocks, BF16), jax...]
where the time goes in v3:
time: 90.4 us; the launch traced here: 90.3 us
  Pallas kernels  89.5 us (99%)
    pallas_call x1, Pallas kernels, shards(): pl.pallas_call(kernel, out_shape=(jax.ShapeDtypeStruct(blocks, BF16), jax...  87.2 us
    pallas_call x1, Pallas kernels, shards(): pl.pallas_call(finish, out_shape=tuple((jax.ShapeDtypeStruct(a.shape, a.d...  2.3 us

profile of v3, /device:TPU:0, one launch (start us, length us, event | category | flops | bytes accessed | tf_op | source)
XLA Modules:
  0.0 90.3 jit_solution(2511346388429089551)
XLA Ops:
  0.6 87.2 %shard_map.67 = (bf16[32,16,1024]{2,1,0:T(8,128)(2,1)}, f32[8,3072]{1,0:T(8,128)}, f32[8,1024]{1,0:T(8,128)}) custom-call(bf16[32,16,1024]{2,1,0:T(8,128)(2,1)} %bitcast.5, bf16[1024,3072]{1,0:T(8,128)(2,1)} %w_qkv.1, bf16[1024,1024]{1,0:T(8,128)(2,1)} %w_out.1, bf16[32,16,1024]{2,1,0:T(8,128)(2,1)} %bitcast.6), custom_call_target="tpu_custom_call" | custom-call | flops 12000000000 | bytes 12582912 | tf_op jit(solution)/shard_map/pallas_call | solution.py:361
  87.8 2.3 %shard_map.68 = (bf16[32,16,1024]{2,1,0:T(8,128)(2,1)}, f32[8,3072]{1,0:T(8,128)}, f32[8,1024]{1,0:T(8,128)}) custom-call(bf16[32,16,1024]{2,1,0:T(8,128)(2,1)} %get-tuple-element.9.refs_0_, f32[8,3072]{1,0:T(8,128)} %get-tuple-element.10.refs_1_, f32[8,1024]{1,0:T(8,128)} %get-tuple-element.11.refs_2_), custom_call_target="tpu_custom_call" | custom-call | tf_op jit(solution)/shard_map/pallas_call | solution.py:417
